TPU v7x, 256 devices: a whole 4x4x8 slice. The times are simulated.
256 devices in a mesh: shot: 8 (over y, core), gx: 4 (over z_hi), gy: 8 (over z_lo, x).
Axes of the slice: x: 4, y: 4, z: 8 (z_hi: 4, z_lo: 2; z = z_hi * 2 + z_lo), core: 2. Of those that a mesh axis runs over, the one named last changes fastest.
Arguments:
- latent: float32 [32, 24, 4096], P('shot', 'gx', 'gy'), may hold values from -6 to 6
- w_first: float32 [64, 64], replicated, may hold values from -0.75 to 0.75
- w_second: float32 [64, 128], replicated, may hold values from -0.75 to 0.75
- fwd_press: float32 [8, 96, 256, 128], P('shot', 'gx', 'gy'), may hold values from -1.5 to 8
- fwd_vel: float32 [8, 3, 96, 256, 128], P('shot', None, 'gx', 'gy'), may hold values from -1.5 to 8
- adj_press: float32 [8, 96, 256, 128], P('shot', 'gx', 'gy'), may hold values from -1.5 to 8
- adj_vel: float32 [8, 3, 96, 256, 128], P('shot', None, 'gx', 'gy'), may hold values from -1.5 to 8
- src_pos: int32 [3, 8], P(None, 'shot'), may hold values from 0 to 255, as said below
- src_amp: float32 [3, 8], P(None, 'shot'), may hold values from -24 to 24
- rec_pos: int32 [8, 3, 2048], P('shot'), may hold values from 0 to 255, as said below
- observed: float32 [8, 3, 2048], P('shot'), may hold values from -6 to 6
Outputs:
- grad_latent: float32 [32, 24, 4096], P('shot', 'gx', 'gy')
- grad_first: float32 [64, 64], replicated
- grad_second: float32 [64, 128], replicated
Inputs may be any that keep to these rules, and one draw needn't show every extreme that they name: `src_pos`: row 0 is an x cell below 96, row 1 a y cell below 256, row 2 a depth cell below 128. `rec_pos`: component 0 is an x cell below 96, component 1 a y cell below 256, component 2 a depth cell below 128; cells may repeat.
All inputs are finite; a program needn't handle non-finite values.
Results may differ from a plain program's by a relative error of at most 0.0003.
Values sent between devices are 32-bit elements; how exact they have to be, the bound alone decides.
No kernel may reach another device: no remote copies, remote signals or barrier semaphores. Data moves between devices by JAX's collectives and lax.ppermute only.
A program may use at most 64 MiB of HBM per device.

v0:
```python
import jax
import jax.numpy as jnp
from jax import lax
from jax.sharding import PartitionSpec as P

CH = 64
STEPS = 3
coeffs = (1225.0 / 1024.0, -245.0 / 3072.0, 49.0 / 5120.0, -5.0 / 7168.0)


def with_halo(block, sides, width):
    for axis, dim in sides:
        count = lax.axis_size(axis)
        forward = [(i, i + 1) for i in range(count - 1)]
        backward = [(target, source) for source, target in forward]
        low = lax.ppermute(
            lax.slice_in_dim(block, block.shape[dim] - width, None, axis=dim), axis, forward
        )
        high = lax.ppermute(lax.slice_in_dim(block, 0, width, axis=dim), axis, backward)
        block = jnp.concatenate([low, block, high], axis=dim)
    return block


def take_slab(values_in, axis_id, start_at, length):
    return lax.slice_in_dim(values_in, start_at, start_at + length, axis=axis_id)


def diff_plus(extended, axis_id, start_at, length):
    summed = 0.0
    for order, weight in enumerate(coeffs):
        offset = order + 1
        summed = summed + weight * (
            take_slab(extended, axis_id, start_at + offset, length)
            - take_slab(extended, axis_id, start_at - offset + 1, length)
        )
    return summed


def diff_minus(extended, axis_id, start_at, length):
    summed = 0.0
    for order, weight in enumerate(coeffs):
        offset = order + 1
        summed = summed + weight * (
            take_slab(extended, axis_id, start_at + offset - 1, length)
            - take_slab(extended, axis_id, start_at - offset, length)
        )
    return summed


def depth_pad(field_in):
    return jnp.pad(field_in, ((0, 0), (0, 0), (4, 4)))


def rim_x(field_in):
    return with_halo(field_in, (("gx", 0),), 4)


def rim_y(field_in):
    return with_halo(field_in, (("gy", 1),), 4)


def narrow_step(fields, modulus, buoyancy):
    pressure, vel_x, vel_y, vel_z = fields
    size_x, size_y, size_z = pressure.shape
    extended = with_halo(pressure, (("gx", 0), ("gy", 1)), 4)
    grad_x = diff_plus(extended[:, 4 : 4 + size_y], 0, 4, size_x)
    grad_y = diff_plus(extended[4 : 4 + size_x], 1, 4, size_y)
    grad_z = diff_plus(depth_pad(pressure), 2, 4, size_z)
    vel_x = vel_x - buoyancy * grad_x
    vel_y = vel_y - buoyancy * grad_y
    vel_z = vel_z - buoyancy * grad_z
    diverge = (
        diff_minus(rim_x(vel_x), 0, 4, size_x)
        + diff_minus(rim_y(vel_y), 1, 4, size_y)
        + diff_minus(depth_pad(vel_z), 2, 4, size_z)
    )
    pressure = pressure - modulus * diverge
    return (
        (pressure, vel_x, vel_y, vel_z),
        diverge,
        (grad_x, grad_y, grad_z),
        (vel_x, vel_y, vel_z),
    )


def decode(latent, w_first, w_second):
    depth_c, rows_x, merged = latent.shape
    rows_y = merged // CH
    flattened = latent.reshape(-1, CH)
    hidden = jnp.tanh(jnp.dot(flattened, w_first, precision=lax.Precision.HIGHEST))
    outputs = jnp.dot(hidden, w_second, precision=lax.Precision.HIGHEST)
    fine_out = (
        outputs.reshape(depth_c, rows_x, rows_y, 2, 4, 4, 4)
        .transpose(3, 1, 4, 2, 5, 0, 6)
        .reshape(2, rows_x * 4, rows_y * 4, depth_c * 4)
    )
    return (flattened, hidden, fine_out)


def materials(fine_out):
    wave_speed = 0.15 + 0.25 * jax.nn.sigmoid(fine_out[0])
    density = 1.0 + 1.5 * jax.nn.sigmoid(fine_out[1])
    return (density * wave_speed * wave_speed, 1.0 / density)


def decoder_grads(flattened, hidden, fine_out, grad_mod, grad_buoy, w_first, w_second):
    sig_speed = jax.nn.sigmoid(fine_out[0])
    sig_dens = jax.nn.sigmoid(fine_out[1])
    wave_speed = 0.15 + 0.25 * sig_speed
    density = 1.0 + 1.5 * sig_dens
    grad_speed = grad_mod * 2.0 * density * wave_speed
    grad_dens = grad_mod * wave_speed * wave_speed - grad_buoy / (density * density)
    grad_fine = jnp.stack(
        [
            grad_speed * 0.25 * sig_speed * (1.0 - sig_speed),
            grad_dens * 1.5 * sig_dens * (1.0 - sig_dens),
        ]
    )
    size_x, size_y, size_z = (grad_fine.shape[1], grad_fine.shape[2], grad_fine.shape[3])
    grad_out = (
        grad_fine.reshape(2, size_x // 4, 4, size_y // 4, 4, size_z // 4, 4)
        .transpose(5, 1, 3, 0, 2, 4, 6)
        .reshape(-1, 128)
    )
    grad_hidden = jnp.dot(grad_out, w_second.T, precision=lax.Precision.HIGHEST)
    grad_pre = grad_hidden * (1.0 - hidden * hidden)
    grad_latent = jnp.dot(grad_pre, w_first.T, precision=lax.Precision.HIGHEST).reshape(
        size_z // 4, size_x // 4, size_y // 4 * CH
    )
    grad_second = jnp.dot(hidden.T, grad_out, precision=lax.Precision.HIGHEST)
    grad_first = jnp.dot(flattened.T, grad_pre, precision=lax.Precision.HIGHEST)
    return (grad_latent, grad_first, grad_second)


def locate(positions, anchor_x, anchor_y, size_x, size_y):
    local_x = positions[0] - anchor_x
    local_y = positions[1] - anchor_y
    inside = (local_x >= 0) & (local_x < size_x) & (local_y >= 0) & (local_y < size_y)
    return (
        jnp.clip(local_x, 0, size_x - 1),
        jnp.clip(local_y, 0, size_y - 1),
        positions[2],
        inside,
    )


def body(
    latent,
    w_first,
    w_second,
    fwd_press,
    fwd_vel,
    adj_press,
    adj_vel,
    src_pos,
    src_amp,
    rec_pos,
    observed,
):
    size_x, size_y = (fwd_press.shape[1], fwd_press.shape[2])
    anchor_x = lax.axis_index("gx") * size_x
    anchor_y = lax.axis_index("gy") * size_y
    flattened, hidden, fine_out = decode(latent, w_first, w_second)
    slab_mod, slab_buoy = materials(fine_out)
    stacked = lax.all_gather(jnp.stack([slab_mod, slab_buoy]), "shot", axis=3, tiled=True)
    modulus, buoyancy = (stacked[0], stacked[1])

    def prepare(vel_x, vel_y):
        return (vel_x, vel_y)

    def advance(fields):
        return narrow_step(fields, modulus, buoyancy)

    def one_shot(totals, inputs):
        grad_mod, grad_buoy = totals
        (
            start_press,
            start_vel,
            back_press,
            back_vel,
            source,
            amplitudes,
            receivers,
            observed_now,
        ) = inputs
        src_x, src_y, src_z, src_in = locate(source, anchor_x, anchor_y, size_x, size_y)
        rec_x, rec_y, rec_z, rec_in = locate(receivers, anchor_x, anchor_y, size_x, size_y)
        fields = (start_press,) + prepare(start_vel[0], start_vel[1]) + (start_vel[2],)
        stored = []
        misfits = []
        for moment in range(STEPS):
            fields, diverge, slopes, own_vel = advance(fields)
            pressure = (
                fields[0].at[src_x, src_y, src_z].add(jnp.where(src_in, amplitudes[moment], 0.0))
            )
            fields = (pressure,) + fields[1:]
            misfits.append(
                jnp.where(rec_in, pressure[rec_x, rec_y, rec_z] - observed_now[moment], 0.0)
            )
            stored.append((diverge, slopes))
        fields = (back_press,) + prepare(back_vel[0], back_vel[1]) + (back_vel[2],)
        for moment in reversed(range(STEPS)):
            pressure = fields[0].at[rec_x, rec_y, rec_z].add(misfits[moment])
            fields, diverge, slopes, own_vel = advance((pressure,) + fields[1:])
            grad_mod = grad_mod - fields[0] * stored[moment][0]
            grad_buoy = grad_buoy - (
                own_vel[0] * stored[moment][1][0]
                + own_vel[1] * stored[moment][1][1]
                + own_vel[2] * stored[moment][1][2]
            )
        return ((grad_mod, grad_buoy), None)

    zeros = jnp.zeros(modulus.shape, jnp.float32)
    totals, _ignored = lax.scan(
        one_shot,
        (zeros, zeros),
        (fwd_press, fwd_vel, adj_press, adj_vel, src_pos.T, src_amp.T, rec_pos, observed),
    )
    shares = lax.psum_scatter(
        jnp.stack([totals[0], totals[1]]), "shot", scatter_dimension=3, tiled=True
    )
    grad_latent, grad_first, grad_second = decoder_grads(
        flattened, hidden, fine_out, shares[0], shares[1], w_first, w_second
    )
    grad_first, grad_second = lax.psum((grad_first, grad_second), ("shot", "gx", "gy"))
    return (grad_latent, grad_first, grad_second)


def solution(mesh):
    in_specs = (
        P("shot", "gx", "gy"),
        P(),
        P(),
        P("shot", "gx", "gy", None),
        P("shot", None, "gx", "gy", None),
        P("shot", "gx", "gy", None),
        P("shot", None, "gx", "gy", None),
        P(None, "shot"),
        P(None, "shot"),
        P("shot", None, None),
        P("shot", None, None),
    )
    out_specs = (P("shot", "gx", "gy"), P(), P())
    return jax.shard_map(body, mesh=mesh, in_specs=in_specs, out_specs=out_specs, check_vma=False)
```

profile of v0, /device:TPU:1, one launch (start us, length us, event | category | flops | bytes accessed | tf_op | source)
XLA Modules:
  0.0 564.5 jit_solution(9128224476889360385)
XLA Ops:
  8.8 6.3 %collective-permute-start.1 = (f32[4,32,128]{2,1,0:T(8,128)}, f32[4,32,128]{2,1,0:T(8,128)}, u32[]{:S(2)}, u32[]{:S(2)}) collective-permute-start(f32[4,32,128]{2,1,0:T(8,128)} %get-tuple-element.217), channel_id=1, source_target_pairs={{0,8},{8,16},{16,24},{1,9},{9,17},{17,25},{2,10},{10,18},{18,26},{... | collective-permute-start | bytes 196616 | tf_op jit(solution)/shard_map/while/body/eval_jaxpr/ppermute | solution.py:16
  35.5 20.7 %all_gather.3 = f32[2,24,32,128]{2,1,0,3:T(8,128)S(1)} all-gather(f32[2,24,32,16]{2,1,0,3:T(8,128)S(1)} %copy.37), channel_id=1, replica_groups=mesh['shot'=8,'gx'=4,'gy'=8] {'shot'}, dimensions={3}, use_global_device_ids=true | all-gather | bytes 884736 | tf_op jit(solution)/shard_map/all_gather | solution.py:165
  69.6 6.8 %collective-permute-start.2 = (f32[4,32,128]{2,1,0:T(8,128)S(1)}, f32[4,32,128]{2,1,0:T(8,128)S(1)}, u32[]{:S(2)}, u32[]{:S(2)}) collective-permute-start(f32[4,32,128]{2,1,0:T(8,128)S(1)} %get-tuple-element.214), channel_id=1, source_target_pairs={{0,8},{8,16},{16,24},{1,9},{9,17},{17,25},{2,10},{10,18},{18,26},{... | collective-permute-start | bytes 196616 | tf_op jit(solution)/shard_map/while/body/eval_jaxpr/ppermute | solution.py:16
  93.1 5.5 collective-permute-start.9
  120.4 6.6 %collective-permute-start.10 = (f32[4,32,128]{2,1,0:T(8,128)S(1)}, f32[4,32,128]{2,1,0:T(8,128)S(1)}, u32[]{:S(2)}, u32[]{:S(2)}) collective-permute-start(f32[4,32,128]{2,1,0:T(8,128)S(1)} %get-tuple-element.208), channel_id=1, source_target_pairs={{0,8},{8,16},{16,24},{1,9},{9,17},{17,25},{2,10},{10,18},{18,26},{... | collective-permute-start | bytes 196616 | tf_op jit(solution)/shard_map/while/body/eval_jaxpr/ppermute | solution.py:16
  132.9 5.5 collective-permute-start.17
  146.4 6.1 %collective-permute-start.21 = (f32[32,4,128]{2,1,0:T(4,128)S(1)}, f32[32,4,128]{2,1,0:T(4,128)S(1)}, u32[]{:S(2)}, u32[]{:S(2)}) collective-permute-start(f32[32,4,128]{2,1,0:T(4,128)S(1)} %get-tuple-element.172), channel_id=1, source_target_pairs={{0,1},{1,2},{2,3},{3,4},{4,5},{5,6},{6,7},{8,9},{9,10},{10,11},{11... | collective-permute-start | bytes 196616 | tf_op jit(solution)/shard_map/while/body/eval_jaxpr/ppermute | solution.py:16
  153.2 25.6 %gather_fusion.2 = f32[2048]{0:T(1024)} fusion(f32[24,32,128]{2,1,0:T(8,128)S(1)} %scatter-add.39, s32[2048]{0:T(1024)S(1)} %bitcast.153), kind=kCustom, calls=%fused_computation.2 | custom fusion | bytes 40960 | tf_op jit(solution)/shard_map/while/body/eval_jaxpr/gather | solution.py:198
  183.5 7.1 %collective-permute-start.22 = (f32[24,4,128]{2,1,0:T(4,128)S(1)}, f32[24,4,128]{2,1,0:T(4,128)}, u32[]{:S(2)}, u32[]{:S(2)}) collective-permute-start(f32[24,4,128]{2,1,0:T(4,128)S(1)} %get-tuple-element.204), channel_id=1, source_target_pairs={{0,1},{1,2},{2,3},{3,4},{4,5},{5,6},{6,7},{8,9},{9,10},{10,11},{11... | collective-permute-start | bytes 147464 | tf_op jit(solution)/shard_map/while/body/eval_jaxpr/ppermute | solution.py:16
  192.0 6.1 %collective-permute-start.18 = (f32[4,32,128]{2,1,0:T(8,128)S(1)}, f32[4,32,128]{2,1,0:T(8,128)S(1)}, u32[]{:S(2)}, u32[]{:S(2)}) collective-permute-start(f32[4,32,128]{2,1,0:T(8,128)S(1)} %get-tuple-element.202), channel_id=1, source_target_pairs={{0,8},{8,16},{16,24},{1,9},{9,17},{17,25},{2,10},{10,18},{18,26},{... | collective-permute-start | bytes 196616 | tf_op jit(solution)/shard_map/while/body/eval_jaxpr/ppermute | solution.py:16
  199.6 16.9 %gather_fusion.1 = f32[2048]{0:T(1024)S(1)} fusion(f32[24,32,128]{2,1,0:T(8,128)S(1)} %scatter-add.40, s32[2048]{0:T(1024)S(1)} %bitcast.154), kind=kCustom, calls=%fused_computation.1 | custom fusion | bytes 40960 | tf_op jit(solution)/shard_map/while/body/eval_jaxpr/gather | solution.py:198
  221.7 16.9 %gather_fusion = f32[2048]{0:T(1024)S(1)} fusion(f32[24,32,128]{2,1,0:T(8,128)S(1)} %scatter-add.41, s32[2048]{0:T(1024)S(1)} %bitcast.155), kind=kCustom, calls=%fused_computation | custom fusion | bytes 40960 | tf_op jit(solution)/shard_map/while/body/eval_jaxpr/gather | solution.py:198
  239.3 12.0 %scatter_fusion = f32[98304]{0:T(1024)S(1)} fusion(f32[98304]{0:T(1024)S(1)} %bitcast.161, s32[2048]{0:T(1024)S(1)} %broadcast_select_fusion, f32[2048]{0:T(1024)S(1)} %get-tuple-element.227), kind=kCustom, calls=%fused_computation.3 | custom fusion | flops 2048 | bytes 32768
  263.8 5.5 collective-permute-start.29
  288.0 12.0 %scatter_fusion.1 = f32[98304]{0:T(1024)S(1)} fusion(f32[98304]{0:T(1024)S(1)} %copy.62, s32[2048]{0:T(1024)S(1)} %broadcast_select_fusion, f32[2048]{0:T(1024)S(1)} %copy-done.34), kind=kCustom, calls=%fused_computation.4 | custom fusion | flops 2048 | bytes 32768
  309.0 6.5 %collective-permute-start.37 = (f32[32,4,128]{2,1,0:T(4,128)S(1)}, f32[32,4,128]{2,1,0:T(4,128)S(1)}, u32[]{:S(2)}, u32[]{:S(2)}) collective-permute-start(f32[32,4,128]{2,1,0:T(4,128)S(1)} %get-tuple-element.164), channel_id=1, source_target_pairs={{0,1},{1,2},{2,3},{3,4},{4,5},{5,6},{6,7},{8,9},{9,10},{10,11},{11... | collective-permute-start | bytes 196616 | tf_op jit(solution)/shard_map/while/body/eval_jaxpr/ppermute | solution.py:16
  317.5 5.8 %collective-permute-start.38 = (f32[24,4,128]{2,1,0:T(4,128)S(1)}, f32[24,4,128]{2,1,0:T(4,128)S(1)}, u32[]{:S(2)}, u32[]{:S(2)}) collective-permute-start(f32[24,4,128]{2,1,0:T(4,128)S(1)} %get-tuple-element.189), channel_id=1, source_target_pairs={{0,1},{1,2},{2,3},{3,4},{4,5},{5,6},{6,7},{8,9},{9,10},{10,11},{11... | collective-permute-start | bytes 147464 | tf_op jit(solution)/shard_map/while/body/eval_jaxpr/ppermute | solution.py:16
  337.4 12.0 %scatter_fusion.2 = f32[98304]{0:T(1024)S(1)} fusion(f32[98304]{0:T(1024)S(1)} %copy.63, s32[2048]{0:T(1024)S(1)} %broadcast_select_fusion, f32[2048]{0:T(1024)S(1)} %copy-done.33), kind=kCustom, calls=%fused_computation.5 | custom fusion | flops 2048 | bytes 32768
  362.0 6.7 %collective-permute-start.45 = (f32[32,4,128]{2,1,0:T(4,128)S(1)}, f32[32,4,128]{2,1,0:T(4,128)S(1)}, u32[]{:S(2)}, u32[]{:S(2)}) collective-permute-start(f32[32,4,128]{2,1,0:T(4,128)S(1)} %get-tuple-element.160), channel_id=1, source_target_pairs={{0,1},{1,2},{2,3},{3,4},{4,5},{5,6},{6,7},{8,9},{9,10},{10,11},{11... | collective-permute-start | bytes 196616 | tf_op jit(solution)/shard_map/while/body/eval_jaxpr/ppermute | solution.py:16
  377.4 5.7 %collective-permute-start.46 = (f32[24,4,128]{2,1,0:T(4,128)S(1)}, f32[24,4,128]{2,1,0:T(4,128)S(1)}, u32[]{:S(2)}, u32[]{:S(2)}) collective-permute-start(f32[24,4,128]{2,1,0:T(4,128)S(1)} %get-tuple-element.183), channel_id=1, source_target_pairs={{0,1},{1,2},{2,3},{3,4},{4,5},{5,6},{6,7},{8,9},{9,10},{10,11},{11... | collective-permute-start | bytes 147464 | tf_op jit(solution)/shard_map/while/body/eval_jaxpr/ppermute | solution.py:16
  384.6 5.7 %collective-permute-done.47 = f32[24,4,128]{2,1,0:T(4,128)S(1)} collective-permute-done((f32[24,4,128]{2,1,0:T(4,128)S(1)}, f32[24,4,128]{2,1,0:T(4,128)S(1)}, u32[]{:S(2)}, u32[]{:S(2)}) %collective-permute-start.47) | collective-permute-done | bytes 49184 | tf_op jit(solution)/shard_map/while/body/eval_jaxpr/ppermute | solution.py:19
  393.6 64.4 %reduce-scatter.2.cloned.1.call-done = f32[2,24,32,16]{2,1,0,3:T(8,128)} async-done(((f32[2,24,32,128]{2,1,0,3:T(8,128)}), f32[2,24,32,16]{2,1,0,3:T(8,128)}) %reduce-scatter.2.cloned.1.call-update) | async-done | bytes 98320 | tf_op jit(solution)/shard_map/reduce_scatter | solution.py:219
  464.8 8.5 %copy.43 = f32[4,6,8,2,4,4,4]{2,1,0,6,5,4,3:T(8,128)} copy(f32[4,6,8,2,4,4,4]{5,2,6,0,4,1,3:T(8,128)S(1)} %maximum_bitcast_fusion) | data formatting | bytes 196608 | tf_op jit(solution)/shard_map/transpose | solution.py:122
  477.0 79.0 %all-reduce.12 = (f32[64,64]{0,1:T(8,128)S(1)}, f32[64,128]{1,0:T(8,128)}) all-reduce(f32[64,64]{0,1:T(8,128)S(1)} %convolution_bitcast_fusion, f32[64,128]{1,0:T(8,128)S(1)} %fusion.561), channel_id=1, replica_groups=mesh['shot'=8,'gx'=4,'gy'=8] {'shot','gx','gy'}, use_global_device_ids=true, to_apply=%region_5.6 | all-reduce | flops 12288 | bytes 98304 | tf_op jit(solution)/shard_map/psum | solution.py:225
  (272 shorter events, 184.2 us)
Async XLA Ops:
  7.2 450.8 %reduce-scatter.2.cloned.1.call-start = ((), (), s32[]{:S(2)}) async-start(), calls=%async_computation.1 | async-start | bytes 3538944 | tf_op jit(solution)/shard_map/reduce_scatter | solution.py:219
  8.8 50.7 %collective-permute-start.1 = (f32[4,32,128]{2,1,0:T(8,128)}, f32[4,32,128]{2,1,0:T(8,128)}, u32[]{:S(2)}, u32[]{:S(2)}) collective-permute-start(f32[4,32,128]{2,1,0:T(8,128)} %get-tuple-element.217), channel_id=1, source_target_pairs={{0,8},{8,16},{16,24},{1,9},{9,17},{17,25},{2,10},{10,18},{18,26},{... | collective-permute-start | bytes 196616 | tf_op jit(solution)/shard_map/while/body/eval_jaxpr/ppermute | solution.py:16
  15.1 44.3 %collective-permute-start = (f32[4,32,128]{2,1,0:T(8,128)}, f32[4,32,128]{2,1,0:T(8,128)}, u32[]{:S(2)}, u32[]{:S(2)}) collective-permute-start(f32[4,32,128]{2,1,0:T(8,128)} %get-tuple-element.218), channel_id=1, source_target_pairs={{8,0},{16,8},{24,16},{9,1},{17,9},{25,17},{10,2},{18,10},{26,18},{... | collective-permute-start | bytes 196616 | tf_op jit(solution)/shard_map/while/body/eval_jaxpr/ppermute | solution.py:19
  60.2 16.2 %collective-permute-start.4 = (f32[32,4,128]{2,1,0:T(4,128)S(1)}, f32[32,4,128]{2,1,0:T(4,128)S(1)}, u32[]{:S(2)}, u32[]{:S(2)}) collective-permute-start(f32[32,4,128]{2,1,0:T(4,128)S(1)} %get-tuple-element.179), channel_id=1, source_target_pairs={{1,0},{2,1},{3,2},{4,3},{5,4},{6,5},{7,6},{9,8},{10,9},{11,10},{12... | collective-permute-start | bytes 196616 | tf_op jit(solution)/shard_map/while/body/eval_jaxpr/ppermute | solution.py:19
  61.5 14.9 %collective-permute-start.5 = (f32[32,4,128]{2,1,0:T(4,128)S(1)}, f32[32,4,128]{2,1,0:T(4,128)S(1)}, u32[]{:S(2)}, u32[]{:S(2)}) collective-permute-start(f32[32,4,128]{2,1,0:T(4,128)S(1)} %get-tuple-element.180), channel_id=1, source_target_pairs={{0,1},{1,2},{2,3},{3,4},{4,5},{5,6},{6,7},{8,9},{9,10},{10,11},{11... | collective-permute-start | bytes 196616 | tf_op jit(solution)/shard_map/while/body/eval_jaxpr/ppermute | solution.py:16
  68.3 20.4 %collective-permute-start.3 = (f32[4,32,128]{2,1,0:T(8,128)S(1)}, f32[4,32,128]{2,1,0:T(8,128)S(1)}, u32[]{:S(2)}, u32[]{:S(2)}) collective-permute-start(f32[4,32,128]{2,1,0:T(8,128)S(1)} %get-tuple-element.213), channel_id=1, source_target_pairs={{8,0},{16,8},{24,16},{9,1},{17,9},{25,17},{10,2},{18,10},{26,18},{... | collective-permute-start | bytes 196616 | tf_op jit(solution)/shard_map/while/body/eval_jaxpr/ppermute | solution.py:19
  69.6 19.1 %collective-permute-start.2 = (f32[4,32,128]{2,1,0:T(8,128)S(1)}, f32[4,32,128]{2,1,0:T(8,128)S(1)}, u32[]{:S(2)}, u32[]{:S(2)}) collective-permute-start(f32[4,32,128]{2,1,0:T(8,128)S(1)} %get-tuple-element.214), channel_id=1, source_target_pairs={{0,8},{8,16},{16,24},{1,9},{9,17},{17,25},{2,10},{10,18},{18,26},{... | collective-permute-start | bytes 196616 | tf_op jit(solution)/shard_map/while/body/eval_jaxpr/ppermute | solution.py:16
  79.6 9.1 %collective-permute-start.7 = (f32[24,4,128]{2,1,0:T(4,128)S(1)}, f32[24,4,128]{2,1,0:T(4,128)S(1)}, u32[]{:S(2)}, u32[]{:S(2)}) collective-permute-start(f32[24,4,128]{2,1,0:T(4,128)S(1)} %get-tuple-element.215), channel_id=1, source_target_pairs={{1,0},{2,1},{3,2},{4,3},{5,4},{6,5},{7,6},{9,8},{10,9},{11,10},{12... | collective-permute-start | bytes 147464 | tf_op jit(solution)/shard_map/while/body/eval_jaxpr/ppermute | solution.py:19
  112.7 15.8 %collective-permute-start.15 = (f32[24,4,128]{2,1,0:T(4,128)S(1)}, f32[24,4,128]{2,1,0:T(4,128)S(1)}, u32[]{:S(2)}, u32[]{:S(2)}) collective-permute-start(f32[24,4,128]{2,1,0:T(4,128)S(1)} %get-tuple-element.209), channel_id=1, source_target_pairs={{1,0},{2,1},{3,2},{4,3},{5,4},{6,5},{7,6},{9,8},{10,9},{11,10},{12... | collective-permute-start | bytes 147464 | tf_op jit(solution)/shard_map/while/body/eval_jaxpr/ppermute | solution.py:19
  114.0 14.5 %collective-permute-start.14 = (f32[24,4,128]{2,1,0:T(4,128)S(1)}, f32[24,4,128]{2,1,0:T(4,128)S(1)}, u32[]{:S(2)}, u32[]{:S(2)}) collective-permute-start(f32[24,4,128]{2,1,0:T(4,128)S(1)} %get-tuple-element.210), channel_id=1, source_target_pairs={{0,1},{1,2},{2,3},{3,4},{4,5},{5,6},{6,7},{8,9},{9,10},{10,11},{11... | collective-permute-start | bytes 147464 | tf_op jit(solution)/shard_map/while/body/eval_jaxpr/ppermute | solution.py:16
  119.1 9.4 %collective-permute-start.11 = (f32[4,32,128]{2,1,0:T(8,128)S(1)}, f32[4,32,128]{2,1,0:T(8,128)S(1)}, u32[]{:S(2)}, u32[]{:S(2)}) collective-permute-start(f32[4,32,128]{2,1,0:T(8,128)S(1)} %get-tuple-element.207), channel_id=1, source_target_pairs={{8,0},{16,8},{24,16},{9,1},{17,9},{25,17},{10,2},{18,10},{26,18},{... | collective-permute-start | bytes 196616 | tf_op jit(solution)/shard_map/while/body/eval_jaxpr/ppermute | solution.py:19
  120.4 8.1 %collective-permute-start.10 = (f32[4,32,128]{2,1,0:T(8,128)S(1)}, f32[4,32,128]{2,1,0:T(8,128)S(1)}, u32[]{:S(2)}, u32[]{:S(2)}) collective-permute-start(f32[4,32,128]{2,1,0:T(8,128)S(1)} %get-tuple-element.208), channel_id=1, source_target_pairs={{0,8},{8,16},{16,24},{1,9},{9,17},{17,25},{2,10},{10,18},{18,26},{... | collective-permute-start | bytes 196616 | tf_op jit(solution)/shard_map/while/body/eval_jaxpr/ppermute | solution.py:16
  145.1 33.7 %collective-permute-start.20 = (f32[32,4,128]{2,1,0:T(4,128)S(1)}, f32[32,4,128]{2,1,0:T(4,128)S(1)}, u32[]{:S(2)}, u32[]{:S(2)}) collective-permute-start(f32[32,4,128]{2,1,0:T(4,128)S(1)} %get-tuple-element.171), channel_id=1, source_target_pairs={{1,0},{2,1},{3,2},{4,3},{5,4},{6,5},{7,6},{9,8},{10,9},{11,10},{12... | collective-permute-start | bytes 196616 | tf_op jit(solution)/shard_map/while/body/eval_jaxpr/ppermute | solution.py:19
  146.4 32.4 %collective-permute-start.21 = (f32[32,4,128]{2,1,0:T(4,128)S(1)}, f32[32,4,128]{2,1,0:T(4,128)S(1)}, u32[]{:S(2)}, u32[]{:S(2)}) collective-permute-start(f32[32,4,128]{2,1,0:T(4,128)S(1)} %get-tuple-element.172), channel_id=1, source_target_pairs={{0,1},{1,2},{2,3},{3,4},{4,5},{5,6},{6,7},{8,9},{9,10},{10,11},{11... | collective-permute-start | bytes 196616 | tf_op jit(solution)/shard_map/while/body/eval_jaxpr/ppermute | solution.py:16
  182.2 34.3 %collective-permute-start.23 = (f32[24,4,128]{2,1,0:T(4,128)S(1)}, f32[24,4,128]{2,1,0:T(4,128)}, u32[]{:S(2)}, u32[]{:S(2)}) collective-permute-start(f32[24,4,128]{2,1,0:T(4,128)S(1)} %get-tuple-element.203), channel_id=1, source_target_pairs={{1,0},{2,1},{3,2},{4,3},{5,4},{6,5},{7,6},{9,8},{10,9},{11,10},{12... | collective-permute-start | bytes 147464 | tf_op jit(solution)/shard_map/while/body/eval_jaxpr/ppermute | solution.py:19
  183.5 33.0 %collective-permute-start.22 = (f32[24,4,128]{2,1,0:T(4,128)S(1)}, f32[24,4,128]{2,1,0:T(4,128)}, u32[]{:S(2)}, u32[]{:S(2)}) collective-permute-start(f32[24,4,128]{2,1,0:T(4,128)S(1)} %get-tuple-element.204), channel_id=1, source_target_pairs={{0,1},{1,2},{2,3},{3,4},{4,5},{5,6},{6,7},{8,9},{9,10},{10,11},{11... | collective-permute-start | bytes 147464 | tf_op jit(solution)/shard_map/while/body/eval_jaxpr/ppermute | solution.py:16
  190.7 25.8 %collective-permute-start.19 = (f32[4,32,128]{2,1,0:T(8,128)S(1)}, f32[4,32,128]{2,1,0:T(8,128)S(1)}, u32[]{:S(2)}, u32[]{:S(2)}) collective-permute-start(f32[4,32,128]{2,1,0:T(8,128)S(1)} %get-tuple-element.201), channel_id=1, source_target_pairs={{8,0},{16,8},{24,16},{9,1},{17,9},{25,17},{10,2},{18,10},{26,18},{... | collective-permute-start | bytes 196616 | tf_op jit(solution)/shard_map/while/body/eval_jaxpr/ppermute | solution.py:19
  192.0 24.5 %collective-permute-start.18 = (f32[4,32,128]{2,1,0:T(8,128)S(1)}, f32[4,32,128]{2,1,0:T(8,128)S(1)}, u32[]{:S(2)}, u32[]{:S(2)}) collective-permute-start(f32[4,32,128]{2,1,0:T(8,128)S(1)} %get-tuple-element.202), channel_id=1, source_target_pairs={{0,8},{8,16},{16,24},{1,9},{9,17},{17,25},{2,10},{10,18},{18,26},{... | collective-permute-start | bytes 196616 | tf_op jit(solution)/shard_map/while/body/eval_jaxpr/ppermute | solution.py:16
  271.3 12.0 %collective-permute-start.30 = (f32[24,4,128]{2,1,0:T(4,128)S(1)}, f32[24,4,128]{2,1,0:T(4,128)S(1)}, u32[]{:S(2)}, u32[]{:S(2)}) collective-permute-start(f32[24,4,128]{2,1,0:T(4,128)S(1)} %get-tuple-element.195), channel_id=1, source_target_pairs={{0,1},{1,2},{2,3},{3,4},{4,5},{5,6},{6,7},{8,9},{9,10},{10,11},{11... | collective-permute-start | bytes 147464 | tf_op jit(solution)/shard_map/while/body/eval_jaxpr/ppermute | solution.py:16
  317.5 13.8 %collective-permute-start.38 = (f32[24,4,128]{2,1,0:T(4,128)S(1)}, f32[24,4,128]{2,1,0:T(4,128)S(1)}, u32[]{:S(2)}, u32[]{:S(2)}) collective-permute-start(f32[24,4,128]{2,1,0:T(4,128)S(1)} %get-tuple-element.189), channel_id=1, source_target_pairs={{0,1},{1,2},{2,3},{3,4},{4,5},{5,6},{6,7},{8,9},{9,10},{10,11},{11... | collective-permute-start | bytes 147464 | tf_op jit(solution)/shard_map/while/body/eval_jaxpr/ppermute | solution.py:16
  323.4 8.0 %collective-permute-start.39 = (f32[24,4,128]{2,1,0:T(4,128)S(1)}, f32[24,4,128]{2,1,0:T(4,128)S(1)}, u32[]{:S(2)}, u32[]{:S(2)}) collective-permute-start(f32[24,4,128]{2,1,0:T(4,128)S(1)} %get-tuple-element.190), channel_id=1, source_target_pairs={{1,0},{2,1},{3,2},{4,3},{5,4},{6,5},{7,6},{9,8},{10,9},{11,10},{12... | collective-permute-start | bytes 147464 | tf_op jit(solution)/shard_map/while/body/eval_jaxpr/ppermute | solution.py:19
  362.0 8.0 %collective-permute-start.45 = (f32[32,4,128]{2,1,0:T(4,128)S(1)}, f32[32,4,128]{2,1,0:T(4,128)S(1)}, u32[]{:S(2)}, u32[]{:S(2)}) collective-permute-start(f32[32,4,128]{2,1,0:T(4,128)S(1)} %get-tuple-element.160), channel_id=1, source_target_pairs={{0,1},{1,2},{2,3},{3,4},{4,5},{5,6},{6,7},{8,9},{9,10},{10,11},{11... | collective-permute-start | bytes 196616 | tf_op jit(solution)/shard_map/while/body/eval_jaxpr/ppermute | solution.py:16
  373.0 17.3 %collective-permute-start.42 = (f32[4,32,128]{2,1,0:T(8,128)S(1)}, f32[4,32,128]{2,1,0:T(8,128)S(1)}, u32[]{:S(2)}, u32[]{:S(2)}) collective-permute-start(f32[4,32,128]{2,1,0:T(8,128)S(1)} %get-tuple-element.185), channel_id=1, source_target_pairs={{0,8},{8,16},{16,24},{1,9},{9,17},{17,25},{2,10},{10,18},{18,26},{... | collective-permute-start | bytes 196616 | tf_op jit(solution)/shard_map/while/body/eval_jaxpr/ppermute | solution.py:16
  376.0 14.2 %collective-permute-start.43 = (f32[4,32,128]{2,1,0:T(8,128)S(1)}, f32[4,32,128]{2,1,0:T(8,128)S(1)}, u32[]{:S(2)}, u32[]{:S(2)}) collective-permute-start(f32[4,32,128]{2,1,0:T(8,128)S(1)} %get-tuple-element.186), channel_id=1, source_target_pairs={{8,0},{16,8},{24,16},{9,1},{17,9},{25,17},{10,2},{18,10},{26,18},{... | collective-permute-start | bytes 196616 | tf_op jit(solution)/shard_map/while/body/eval_jaxpr/ppermute | solution.py:19
  (71 other events, 941.8 us)
Sparse Core Ops, SparseCore 0:
  393.7 64.2 reduce-scatter.1
where the time goes:
time: 575 us; the launch traced here: 565 us
  starting transfers between devices  160 us (28%)
  waiting for transfers between devices  103 us (18%)
  local copies, waits for them, and re-layouts  99.9 us (17%)
  blocking collectives  99.8 us (17%)
  other arithmetic  72.8 us (13%)
  between operations  26.6 us (5%)
    ppermute x24, starting transfers between devices, with_halo(): lax.ppermute(lax.slice_in_dim(block, block.shape[dim] - width, None, axis...  129 us
    psum x1, blocking collectives, body(): lax.psum((grad_first, grad_second), ('shot', 'gx', 'gy'))  79 us
    reduce_scatter x1, waiting for transfers between devices, body(): lax.psum_scatter(jnp.stack([totals[0], totals[1]]), 'shot', scatter_dimen...  64.4 us
    gather x3, local copies, waits for them, and re-layouts, one_shot(): pressure[rec_x, rec_y, rec_z] - observed_now[moment]  59.3 us
    unnamed x6, other arithmetic  37.3 us
    ppermute x24, waiting for transfers between devices, with_halo(): lax.ppermute(lax.slice_in_dim(block, 0, width, axis=dim), axis, backward)  32.4 us
    ppermute x24, starting transfers between devices, with_halo(): lax.ppermute(lax.slice_in_dim(block, 0, width, axis=dim), axis, backward)  31.2 us
    all_gather x1, blocking collectives, body(): lax.all_gather(jnp.stack([slab_mod, slab_buoy]), 'shot', axis=3, tiled=True)  20.7 us
  transfers between devices with their start and end apart: 49, of which 14 were waited for; matrix products, arithmetic and copies ran while one was open for 14% of the time, Pallas kernels for 0%

commit v1 on v0

--- a/solution.py
+++ b/solution.py
@@ -222,7 +222,10 @@
     grad_latent, grad_first, grad_second = decoder_grads(
         flattened, hidden, fine_out, shares[0], shares[1], w_first, w_second
     )
-    grad_first, grad_second = lax.psum((grad_first, grad_second), ("shot", "gx", "gy"))
+    begin_the_sizes = lambda block_in: lax.psum(
+        lax.psum(block_in, axis_name="shot"), axis_name=("gx", "gy")
+    )
+    grad_first, grad_second = begin_the_sizes((grad_first, grad_second))
     return (grad_latent, grad_first, grad_second)
 
 

time: 575 us -> 665 us (1.16)
  the two profiles are of different devices: /device:TPU:1 before, /device:TPU:0 now
where the time goes in v1:
time: 665 us; the launch traced here: 654 us
  blocking collectives  188 us (28%)
  starting transfers between devices  169 us (25%)
  local copies, waits for them, and re-layouts  100 us (15%)
  waiting for transfers between devices  95.5 us (14%)
  other arithmetic  72.5 us (11%)
  between operations  26.9 us (4%)
    psum x1, blocking collectives, body(): lax.psum(lax.psum(block_in, axis_name='shot'), axis_name=('gx', 'gy'))  144 us
    ppermute x24, starting transfers between devices, with_halo(): lax.ppermute(lax.slice_in_dim(block, block.shape[dim] - width, None, axis...  138 us
    gather x3, local copies, waits for them, and re-layouts, one_shot(): pressure[rec_x, rec_y, rec_z] - observed_now[moment]  59.3 us
    reduce_scatter x1, waiting for transfers between devices, body(): lax.psum_scatter(jnp.stack([totals[0], totals[1]]), 'shot', scatter_dimen...  45.3 us
    ppermute x24, waiting for transfers between devices, with_halo(): lax.ppermute(lax.slice_in_dim(block, 0, width, axis=dim), axis, backward)  40.7 us
    unnamed x6, other arithmetic  37.1 us
    ppermute x24, starting transfers between devices, with_halo(): lax.ppermute(lax.slice_in_dim(block, 0, width, axis=dim), axis, backward)  31 us
    psum x1, blocking collectives, body(): lax.psum(block_in, axis_name='shot')  24.5 us
  transfers between devices with their start and end apart: 49, of which 22 were waited for; matrix products, arithmetic and copies ran while one was open for 12% of the time, Pallas kernels for 0%

profile of v1, /device:TPU:0, one launch (start us, length us, event | category | flops | bytes accessed | tf_op | source)
XLA Modules:
  0.0 654.2 jit_solution(12188504431475423485)
XLA Ops:
  33.2 19.9 %all_gather.3 = f32[2,24,32,128]{2,1,0,3:T(8,128)S(1)} all-gather(f32[2,24,32,16]{2,1,0,3:T(8,128)S(1)} %copy.37), channel_id=1, replica_groups=mesh['shot'=8,'gx'=4,'gy'=8] {'shot'}, dimensions={3}, use_global_device_ids=true | all-gather | bytes 884736 | tf_op jit(solution)/shard_map/all_gather | solution.py:165
  67.1 7.1 %collective-permute-start.2 = (f32[4,32,128]{2,1,0:T(8,128)S(1)}, f32[4,32,128]{2,1,0:T(8,128)S(1)}, u32[]{:S(2)}, u32[]{:S(2)}) collective-permute-start(f32[4,32,128]{2,1,0:T(8,128)S(1)} %get-tuple-element.216), channel_id=1, source_target_pairs={{0,8},{8,16},{16,24},{1,9},{9,17},{17,25},{2,10},{10,18},{18,26},{... | collective-permute-start | bytes 196616 | tf_op jit(solution)/shard_map/while/body/eval_jaxpr/ppermute | solution.py:16
  91.5 6.0 collective-permute-start.9
  121.4 6.6 %collective-permute-start.10 = (f32[4,32,128]{2,1,0:T(8,128)S(1)}, f32[4,32,128]{2,1,0:T(8,128)S(1)}, u32[]{:S(2)}, u32[]{:S(2)}) collective-permute-start(f32[4,32,128]{2,1,0:T(8,128)S(1)} %get-tuple-element.210), channel_id=1, source_target_pairs={{0,8},{8,16},{16,24},{1,9},{9,17},{17,25},{2,10},{10,18},{18,26},{... | collective-permute-start | bytes 196616 | tf_op jit(solution)/shard_map/while/body/eval_jaxpr/ppermute | solution.py:16
  134.2 6.0 collective-permute-start.17
  142.2 6.6 %collective-permute-done.16 = f32[4,32,128]{2,1,0:T(8,128)S(1)} collective-permute-done((f32[4,32,128]{2,1,0:T(8,128)S(1)}, f32[4,32,128]{2,1,0:T(8,128)S(1)}, u32[]{:S(2)}, u32[]{:S(2)}) %collective-permute-start.16) | collective-permute-done | bytes 65568 | tf_op jit(solution)/shard_map/while/body/eval_jaxpr/ppermute | solution.py:19
  150.2 6.6 %collective-permute-start.21 = (f32[32,4,128]{2,1,0:T(4,128)S(1)}, f32[32,4,128]{2,1,0:T(4,128)S(1)}, u32[]{:S(2)}, u32[]{:S(2)}) collective-permute-start(f32[32,4,128]{2,1,0:T(4,128)S(1)} %get-tuple-element.174), channel_id=1, source_target_pairs={{0,1},{1,2},{2,3},{3,4},{4,5},{5,6},{6,7},{8,9},{9,10},{10,11},{11... | collective-permute-start | bytes 196616 | tf_op jit(solution)/shard_map/while/body/eval_jaxpr/ppermute | solution.py:16
  157.4 25.6 %gather_fusion.2 = f32[2048]{0:T(1024)} fusion(f32[24,32,128]{2,1,0:T(8,128)S(1)} %scatter-add.39, s32[2048]{0:T(1024)S(1)} %bitcast.153), kind=kCustom, calls=%fused_computation.2 | custom fusion | bytes 40960 | tf_op jit(solution)/shard_map/while/body/eval_jaxpr/gather | solution.py:198
  187.7 7.9 %collective-permute-start.22 = (f32[24,4,128]{2,1,0:T(4,128)S(1)}, f32[24,4,128]{2,1,0:T(4,128)}, u32[]{:S(2)}, u32[]{:S(2)}) collective-permute-start(f32[24,4,128]{2,1,0:T(4,128)S(1)} %get-tuple-element.206), channel_id=1, source_target_pairs={{0,1},{1,2},{2,3},{3,4},{4,5},{5,6},{6,7},{8,9},{9,10},{10,11},{11... | collective-permute-start | bytes 147464 | tf_op jit(solution)/shard_map/while/body/eval_jaxpr/ppermute | solution.py:16
  197.0 6.7 %collective-permute-start.18 = (f32[4,32,128]{2,1,0:T(8,128)S(1)}, f32[4,32,128]{2,1,0:T(8,128)S(1)}, u32[]{:S(2)}, u32[]{:S(2)}) collective-permute-start(f32[4,32,128]{2,1,0:T(8,128)S(1)} %get-tuple-element.204), channel_id=1, source_target_pairs={{0,8},{8,16},{16,24},{1,9},{9,17},{17,25},{2,10},{10,18},{18,26},{... | collective-permute-start | bytes 196616 | tf_op jit(solution)/shard_map/while/body/eval_jaxpr/ppermute | solution.py:16
  205.2 16.9 %gather_fusion.1 = f32[2048]{0:T(1024)S(1)} fusion(f32[24,32,128]{2,1,0:T(8,128)S(1)} %scatter-add.40, s32[2048]{0:T(1024)S(1)} %bitcast.154), kind=kCustom, calls=%fused_computation.1 | custom fusion | bytes 40960 | tf_op jit(solution)/shard_map/while/body/eval_jaxpr/gather | solution.py:198
  227.4 16.9 %gather_fusion = f32[2048]{0:T(1024)S(1)} fusion(f32[24,32,128]{2,1,0:T(8,128)S(1)} %scatter-add.41, s32[2048]{0:T(1024)S(1)} %bitcast.155), kind=kCustom, calls=%fused_computation | custom fusion | bytes 40960 | tf_op jit(solution)/shard_map/while/body/eval_jaxpr/gather | solution.py:198
  245.0 11.9 %scatter_fusion = f32[98304]{0:T(1024)S(1)} fusion(f32[98304]{0:T(1024)S(1)} %bitcast.161, s32[2048]{0:T(1024)S(1)} %broadcast_select_fusion, f32[2048]{0:T(1024)S(1)} %get-tuple-element.229), kind=kCustom, calls=%fused_computation.3 | custom fusion | flops 2048 | bytes 32768
  298.2 11.9 %scatter_fusion.1 = f32[98304]{0:T(1024)S(1)} fusion(f32[98304]{0:T(1024)S(1)} %copy.62, s32[2048]{0:T(1024)S(1)} %broadcast_select_fusion, f32[2048]{0:T(1024)S(1)} %copy-done.34), kind=kCustom, calls=%fused_computation.4 | custom fusion | flops 2048 | bytes 32768
  320.3 6.9 %collective-permute-start.37 = (f32[32,4,128]{2,1,0:T(4,128)S(1)}, f32[32,4,128]{2,1,0:T(4,128)S(1)}, u32[]{:S(2)}, u32[]{:S(2)}) collective-permute-start(f32[32,4,128]{2,1,0:T(4,128)S(1)} %get-tuple-element.166), channel_id=1, source_target_pairs={{0,1},{1,2},{2,3},{3,4},{4,5},{5,6},{6,7},{8,9},{9,10},{10,11},{11... | collective-permute-start | bytes 196616 | tf_op jit(solution)/shard_map/while/body/eval_jaxpr/ppermute | solution.py:16
  329.8 6.4 collective-permute-start.38
  351.3 11.9 %scatter_fusion.2 = f32[98304]{0:T(1024)S(1)} fusion(f32[98304]{0:T(1024)S(1)} %copy.63, s32[2048]{0:T(1024)S(1)} %broadcast_select_fusion, f32[2048]{0:T(1024)S(1)} %copy-done.33), kind=kCustom, calls=%fused_computation.5 | custom fusion | flops 2048 | bytes 32768
  377.7 8.3 %collective-permute-start.45 = (f32[32,4,128]{2,1,0:T(4,128)S(1)}, f32[32,4,128]{2,1,0:T(4,128)S(1)}, u32[]{:S(2)}, u32[]{:S(2)}) collective-permute-start(f32[32,4,128]{2,1,0:T(4,128)S(1)} %get-tuple-element.162), channel_id=1, source_target_pairs={{0,1},{1,2},{2,3},{3,4},{4,5},{5,6},{6,7},{8,9},{9,10},{10,11},{11... | collective-permute-start | bytes 196616 | tf_op jit(solution)/shard_map/while/body/eval_jaxpr/ppermute | solution.py:16
  395.3 6.1 collective-permute-start.46
  403.1 6.8 %collective-permute-done.47 = f32[24,4,128]{2,1,0:T(4,128)S(1)} collective-permute-done((f32[24,4,128]{2,1,0:T(4,128)S(1)}, f32[24,4,128]{2,1,0:T(4,128)S(1)}, u32[]{:S(2)}, u32[]{:S(2)}) %collective-permute-start.47) | collective-permute-done | bytes 49184 | tf_op jit(solution)/shard_map/while/body/eval_jaxpr/ppermute | solution.py:19
  413.3 45.3 %reduce-scatter.2.cloned.1.call-done = f32[2,24,32,16]{2,1,0,3:T(8,128)} async-done(((f32[2,24,32,128]{2,1,0,3:T(8,128)}), f32[2,24,32,16]{2,1,0,3:T(8,128)}) %reduce-scatter.2.cloned.1.call-update) | async-done | bytes 98320 | tf_op jit(solution)/shard_map/reduce_scatter | solution.py:219
  465.3 8.5 %copy.43 = f32[4,6,8,2,4,4,4]{2,1,0,6,5,4,3:T(8,128)} copy(f32[4,6,8,2,4,4,4]{5,2,6,0,4,1,3:T(8,128)S(1)} %maximum_bitcast_fusion) | data formatting | bytes 196608 | tf_op jit(solution)/shard_map/transpose | solution.py:122
  477.5 24.5 %all-reduce.13 = (f32[64,64]{0,1:T(8,128)S(1)}, f32[64,128]{1,0:T(8,128)S(1)}) all-reduce(f32[64,64]{0,1:T(8,128)S(1)} %convolution_bitcast_fusion, f32[64,128]{1,0:T(8,128)S(1)} %fusion.561), channel_id=1, replica_groups=mesh['shot'=8,'gx'=4,'gy'=8] {'shot'}, use_global_device_ids=true, to_apply=%region_5.6 | all-reduce | flops 12288 | bytes 98304 | tf_op jit(solution)/shard_map/psum | solution.py:226
  502.0 143.5 %all-reduce.12 = (f32[64,64]{0,1:T(8,128)S(1)}, f32[64,128]{1,0:T(8,128)}) all-reduce(f32[64,64]{0,1:T(8,128)S(1)} %get-tuple-element.110, f32[64,128]{1,0:T(8,128)S(1)} %get-tuple-element.111), channel_id=1, replica_groups=mesh['shot'=8,'gx'=4,'gy'=8] {'gx','gy'}, use_global_device_ids=true, to_apply=%region_6.7 | all-reduce | flops 12288 | bytes 98304 | tf_op jit(solution)/shard_map/psum | solution.py:225
  (273 shorter events, 202.5 us)
Async XLA Ops:
  7.2 451.4 %reduce-scatter.2.cloned.1.call-start = ((), (), s32[]{:S(2)}) async-start(), calls=%async_computation.1 | async-start | bytes 3538944 | tf_op jit(solution)/shard_map/reduce_scatter | solution.py:219
  8.7 47.6 %collective-permute-start.1 = (f32[4,32,128]{2,1,0:T(8,128)}, f32[4,32,128]{2,1,0:T(8,128)}, u32[]{:S(2)}, u32[]{:S(2)}) collective-permute-start(f32[4,32,128]{2,1,0:T(8,128)} %get-tuple-element.219), channel_id=1, source_target_pairs={{0,8},{8,16},{16,24},{1,9},{9,17},{17,25},{2,10},{10,18},{18,26},{... | collective-permute-start | bytes 196616 | tf_op jit(solution)/shard_map/while/body/eval_jaxpr/ppermute | solution.py:16
  12.8 43.6 %collective-permute-start = (f32[4,32,128]{2,1,0:T(8,128)}, f32[4,32,128]{2,1,0:T(8,128)}, u32[]{:S(2)}, u32[]{:S(2)}) collective-permute-start(f32[4,32,128]{2,1,0:T(8,128)} %get-tuple-element.220), channel_id=1, source_target_pairs={{8,0},{16,8},{24,16},{9,1},{17,9},{25,17},{10,2},{18,10},{26,18},{... | collective-permute-start | bytes 196616 | tf_op jit(solution)/shard_map/while/body/eval_jaxpr/ppermute | solution.py:19
  57.1 17.0 %collective-permute-start.4 = (f32[32,4,128]{2,1,0:T(4,128)S(1)}, f32[32,4,128]{2,1,0:T(4,128)S(1)}, u32[]{:S(2)}, u32[]{:S(2)}) collective-permute-start(f32[32,4,128]{2,1,0:T(4,128)S(1)} %get-tuple-element.181), channel_id=1, source_target_pairs={{1,0},{2,1},{3,2},{4,3},{5,4},{6,5},{7,6},{9,8},{10,9},{11,10},{12... | collective-permute-start | bytes 196616 | tf_op jit(solution)/shard_map/while/body/eval_jaxpr/ppermute | solution.py:19
  58.4 15.7 %collective-permute-start.5 = (f32[32,4,128]{2,1,0:T(4,128)S(1)}, f32[32,4,128]{2,1,0:T(4,128)S(1)}, u32[]{:S(2)}, u32[]{:S(2)}) collective-permute-start(f32[32,4,128]{2,1,0:T(4,128)S(1)} %get-tuple-element.182), channel_id=1, source_target_pairs={{0,1},{1,2},{2,3},{3,4},{4,5},{5,6},{6,7},{8,9},{9,10},{10,11},{11... | collective-permute-start | bytes 196616 | tf_op jit(solution)/shard_map/while/body/eval_jaxpr/ppermute | solution.py:16
  65.8 21.2 %collective-permute-start.3 = (f32[4,32,128]{2,1,0:T(8,128)S(1)}, f32[4,32,128]{2,1,0:T(8,128)S(1)}, u32[]{:S(2)}, u32[]{:S(2)}) collective-permute-start(f32[4,32,128]{2,1,0:T(8,128)S(1)} %get-tuple-element.215), channel_id=1, source_target_pairs={{8,0},{16,8},{24,16},{9,1},{17,9},{25,17},{10,2},{18,10},{26,18},{... | collective-permute-start | bytes 196616 | tf_op jit(solution)/shard_map/while/body/eval_jaxpr/ppermute | solution.py:19
  67.1 19.9 %collective-permute-start.2 = (f32[4,32,128]{2,1,0:T(8,128)S(1)}, f32[4,32,128]{2,1,0:T(8,128)S(1)}, u32[]{:S(2)}, u32[]{:S(2)}) collective-permute-start(f32[4,32,128]{2,1,0:T(8,128)S(1)} %get-tuple-element.216), channel_id=1, source_target_pairs={{0,8},{8,16},{16,24},{1,9},{9,17},{17,25},{2,10},{10,18},{18,26},{... | collective-permute-start | bytes 196616 | tf_op jit(solution)/shard_map/while/body/eval_jaxpr/ppermute | solution.py:16
  77.4 9.6 %collective-permute-start.7 = (f32[24,4,128]{2,1,0:T(4,128)S(1)}, f32[24,4,128]{2,1,0:T(4,128)S(1)}, u32[]{:S(2)}, u32[]{:S(2)}) collective-permute-start(f32[24,4,128]{2,1,0:T(4,128)S(1)} %get-tuple-element.217), channel_id=1, source_target_pairs={{1,0},{2,1},{3,2},{4,3},{5,4},{6,5},{7,6},{9,8},{10,9},{11,10},{12... | collective-permute-start | bytes 147464 | tf_op jit(solution)/shard_map/while/body/eval_jaxpr/ppermute | solution.py:19
  113.9 15.7 %collective-permute-start.15 = (f32[24,4,128]{2,1,0:T(4,128)S(1)}, f32[24,4,128]{2,1,0:T(4,128)S(1)}, u32[]{:S(2)}, u32[]{:S(2)}) collective-permute-start(f32[24,4,128]{2,1,0:T(4,128)S(1)} %get-tuple-element.211), channel_id=1, source_target_pairs={{1,0},{2,1},{3,2},{4,3},{5,4},{6,5},{7,6},{9,8},{10,9},{11,10},{12... | collective-permute-start | bytes 147464 | tf_op jit(solution)/shard_map/while/body/eval_jaxpr/ppermute | solution.py:19
  115.2 14.4 %collective-permute-start.14 = (f32[24,4,128]{2,1,0:T(4,128)S(1)}, f32[24,4,128]{2,1,0:T(4,128)S(1)}, u32[]{:S(2)}, u32[]{:S(2)}) collective-permute-start(f32[24,4,128]{2,1,0:T(4,128)S(1)} %get-tuple-element.212), channel_id=1, source_target_pairs={{0,1},{1,2},{2,3},{3,4},{4,5},{5,6},{6,7},{8,9},{9,10},{10,11},{11... | collective-permute-start | bytes 147464 | tf_op jit(solution)/shard_map/while/body/eval_jaxpr/ppermute | solution.py:16
  120.1 9.5 %collective-permute-start.11 = (f32[4,32,128]{2,1,0:T(8,128)S(1)}, f32[4,32,128]{2,1,0:T(8,128)S(1)}, u32[]{:S(2)}, u32[]{:S(2)}) collective-permute-start(f32[4,32,128]{2,1,0:T(8,128)S(1)} %get-tuple-element.209), channel_id=1, source_target_pairs={{8,0},{16,8},{24,16},{9,1},{17,9},{25,17},{10,2},{18,10},{26,18},{... | collective-permute-start | bytes 196616 | tf_op jit(solution)/shard_map/while/body/eval_jaxpr/ppermute | solution.py:19
  148.9 34.1 %collective-permute-start.20 = (f32[32,4,128]{2,1,0:T(4,128)S(1)}, f32[32,4,128]{2,1,0:T(4,128)S(1)}, u32[]{:S(2)}, u32[]{:S(2)}) collective-permute-start(f32[32,4,128]{2,1,0:T(4,128)S(1)} %get-tuple-element.173), channel_id=1, source_target_pairs={{1,0},{2,1},{3,2},{4,3},{5,4},{6,5},{7,6},{9,8},{10,9},{11,10},{12... | collective-permute-start | bytes 196616 | tf_op jit(solution)/shard_map/while/body/eval_jaxpr/ppermute | solution.py:19
  150.2 32.8 %collective-permute-start.21 = (f32[32,4,128]{2,1,0:T(4,128)S(1)}, f32[32,4,128]{2,1,0:T(4,128)S(1)}, u32[]{:S(2)}, u32[]{:S(2)}) collective-permute-start(f32[32,4,128]{2,1,0:T(4,128)S(1)} %get-tuple-element.174), channel_id=1, source_target_pairs={{0,1},{1,2},{2,3},{3,4},{4,5},{5,6},{6,7},{8,9},{9,10},{10,11},{11... | collective-permute-start | bytes 196616 | tf_op jit(solution)/shard_map/while/body/eval_jaxpr/ppermute | solution.py:16
  186.4 35.6 %collective-permute-start.23 = (f32[24,4,128]{2,1,0:T(4,128)S(1)}, f32[24,4,128]{2,1,0:T(4,128)}, u32[]{:S(2)}, u32[]{:S(2)}) collective-permute-start(f32[24,4,128]{2,1,0:T(4,128)S(1)} %get-tuple-element.205), channel_id=1, source_target_pairs={{1,0},{2,1},{3,2},{4,3},{5,4},{6,5},{7,6},{9,8},{10,9},{11,10},{12... | collective-permute-start | bytes 147464 | tf_op jit(solution)/shard_map/while/body/eval_jaxpr/ppermute | solution.py:19
  187.7 34.3 %collective-permute-start.22 = (f32[24,4,128]{2,1,0:T(4,128)S(1)}, f32[24,4,128]{2,1,0:T(4,128)}, u32[]{:S(2)}, u32[]{:S(2)}) collective-permute-start(f32[24,4,128]{2,1,0:T(4,128)S(1)} %get-tuple-element.206), channel_id=1, source_target_pairs={{0,1},{1,2},{2,3},{3,4},{4,5},{5,6},{6,7},{8,9},{9,10},{10,11},{11... | collective-permute-start | bytes 147464 | tf_op jit(solution)/shard_map/while/body/eval_jaxpr/ppermute | solution.py:16
  195.7 26.4 %collective-permute-start.19 = (f32[4,32,128]{2,1,0:T(8,128)S(1)}, f32[4,32,128]{2,1,0:T(8,128)S(1)}, u32[]{:S(2)}, u32[]{:S(2)}) collective-permute-start(f32[4,32,128]{2,1,0:T(8,128)S(1)} %get-tuple-element.203), channel_id=1, source_target_pairs={{8,0},{16,8},{24,16},{9,1},{17,9},{25,17},{10,2},{18,10},{26,18},{... | collective-permute-start | bytes 196616 | tf_op jit(solution)/shard_map/while/body/eval_jaxpr/ppermute | solution.py:19
  197.0 25.1 %collective-permute-start.18 = (f32[4,32,128]{2,1,0:T(8,128)S(1)}, f32[4,32,128]{2,1,0:T(8,128)S(1)}, u32[]{:S(2)}, u32[]{:S(2)}) collective-permute-start(f32[4,32,128]{2,1,0:T(8,128)S(1)} %get-tuple-element.204), channel_id=1, source_target_pairs={{0,8},{8,16},{16,24},{1,9},{9,17},{17,25},{2,10},{10,18},{18,26},{... | collective-permute-start | bytes 196616 | tf_op jit(solution)/shard_map/while/body/eval_jaxpr/ppermute | solution.py:16
  279.5 12.6 %collective-permute-start.30 = (f32[24,4,128]{2,1,0:T(4,128)S(1)}, f32[24,4,128]{2,1,0:T(4,128)S(1)}, u32[]{:S(2)}, u32[]{:S(2)}) collective-permute-start(f32[24,4,128]{2,1,0:T(4,128)S(1)} %get-tuple-element.197), channel_id=1, source_target_pairs={{0,1},{1,2},{2,3},{3,4},{4,5},{5,6},{6,7},{8,9},{9,10},{10,11},{11... | collective-permute-start | bytes 147464 | tf_op jit(solution)/shard_map/while/body/eval_jaxpr/ppermute | solution.py:16
  320.3 8.8 %collective-permute-start.37 = (f32[32,4,128]{2,1,0:T(4,128)S(1)}, f32[32,4,128]{2,1,0:T(4,128)S(1)}, u32[]{:S(2)}, u32[]{:S(2)}) collective-permute-start(f32[32,4,128]{2,1,0:T(4,128)S(1)} %get-tuple-element.166), channel_id=1, source_target_pairs={{0,1},{1,2},{2,3},{3,4},{4,5},{5,6},{6,7},{8,9},{9,10},{10,11},{11... | collective-permute-start | bytes 196616 | tf_op jit(solution)/shard_map/while/body/eval_jaxpr/ppermute | solution.py:16
  329.8 15.0 %collective-permute-start.38 = (f32[24,4,128]{2,1,0:T(4,128)S(1)}, f32[24,4,128]{2,1,0:T(4,128)S(1)}, u32[]{:S(2)}, u32[]{:S(2)}) collective-permute-start(f32[24,4,128]{2,1,0:T(4,128)S(1)} %get-tuple-element.191), channel_id=1, source_target_pairs={{0,1},{1,2},{2,3},{3,4},{4,5},{5,6},{6,7},{8,9},{9,10},{10,11},{11... | collective-permute-start | bytes 147464 | tf_op jit(solution)/shard_map/while/body/eval_jaxpr/ppermute | solution.py:16
  376.4 9.9 %collective-permute-start.44 = (f32[32,4,128]{2,1,0:T(4,128)S(1)}, f32[32,4,128]{2,1,0:T(4,128)S(1)}, u32[]{:S(2)}, u32[]{:S(2)}) collective-permute-start(f32[32,4,128]{2,1,0:T(4,128)S(1)} %get-tuple-element.161), channel_id=1, source_target_pairs={{1,0},{2,1},{3,2},{4,3},{5,4},{6,5},{7,6},{9,8},{10,9},{11,10},{12... | collective-permute-start | bytes 196616 | tf_op jit(solution)/shard_map/while/body/eval_jaxpr/ppermute | solution.py:19
  377.7 10.2 %collective-permute-start.45 = (f32[32,4,128]{2,1,0:T(4,128)S(1)}, f32[32,4,128]{2,1,0:T(4,128)S(1)}, u32[]{:S(2)}, u32[]{:S(2)}) collective-permute-start(f32[32,4,128]{2,1,0:T(4,128)S(1)} %get-tuple-element.162), channel_id=1, source_target_pairs={{0,1},{1,2},{2,3},{3,4},{4,5},{5,6},{6,7},{8,9},{9,10},{10,11},{11... | collective-permute-start | bytes 196616 | tf_op jit(solution)/shard_map/while/body/eval_jaxpr/ppermute | solution.py:16
  390.8 19.1 %collective-permute-start.42 = (f32[4,32,128]{2,1,0:T(8,128)S(1)}, f32[4,32,128]{2,1,0:T(8,128)S(1)}, u32[]{:S(2)}, u32[]{:S(2)}) collective-permute-start(f32[4,32,128]{2,1,0:T(8,128)S(1)} %get-tuple-element.187), channel_id=1, source_target_pairs={{0,8},{8,16},{16,24},{1,9},{9,17},{17,25},{2,10},{10,18},{18,26},{... | collective-permute-start | bytes 196616 | tf_op jit(solution)/shard_map/while/body/eval_jaxpr/ppermute | solution.py:16
  394.0 15.9 %collective-permute-start.43 = (f32[4,32,128]{2,1,0:T(8,128)S(1)}, f32[4,32,128]{2,1,0:T(8,128)S(1)}, u32[]{:S(2)}, u32[]{:S(2)}) collective-permute-start(f32[4,32,128]{2,1,0:T(8,128)S(1)} %get-tuple-element.188), channel_id=1, source_target_pairs={{8,0},{16,8},{24,16},{9,1},{17,9},{25,17},{10,2},{18,10},{26,18},{... | collective-permute-start | bytes 196616 | tf_op jit(solution)/shard_map/while/body/eval_jaxpr/ppermute | solution.py:19
  (71 other events, 1001.1 us)
Sparse Core Ops, SparseCore 0:
  413.4 45.1 reduce-scatter.1
